TPU v7x, 32 devices: a whole 2x2x4 slice. The times are simulated.
32 devices in a mesh: dp: 4 (over y, x), tensor: 8 (over z, core).
Axes of the slice: x: 2, y: 2, z: 4, core: 2. Of those that a mesh axis runs over, the one named last changes fastest.
Arguments:
- tokens: bfloat16 [8, 1024, 2048], P('dp', 'tensor'), may hold values from -6 to 6
- cotangent: bfloat16 [8, 1024, 2048], P('dp', 'tensor'), may hold values from -6 to 6
- lengths: int32 [8], P('dp'), may hold values from 256 to 1024, as said below
- ln1_gain: float32 [2048], replicated, may hold values from 0.25 to 1.75
- ln1_shift: float32 [2048], replicated, may hold values from -1.5 to 1.5
- qkv_weight: bfloat16 [3, 2048, 2048], P(None, None, 'tensor'), may hold values from -0.125 to 0.125
- qkv_bias: float32 [2, 2048], P(None, 'tensor'), may hold values from -2.5 to 2.5
- out_weight: bfloat16 [2048, 2048], P('tensor'), may hold values from -1 to 1
- out_bias: float32 [2048], replicated, may hold values from -1.5 to 1.5
- ln2_gain: float32 [2048], replicated, may hold values from 0.25 to 1.75
- ln2_shift: float32 [2048], replicated, may hold values from -1.5 to 1.5
- up_weight: bfloat16 [2048, 8192], P(None, 'tensor'), may hold values from -0.125 to 0.125
- up_bias: float32 [8192], P('tensor'), may hold values from -2.5 to 2.5
- down_weight: bfloat16 [8192, 2048], P('tensor'), may hold values from -0.0625 to 0.0625
- down_bias: float32 [2048], replicated, may hold values from -1.5 to 1.5
Outputs:
- output: bfloat16 [8, 1024, 2048], P('dp', 'tensor')
- input_grad: float32 [8, 1024, 2048], P('dp', 'tensor')
- ln1_gain_grad: float32 [2048], replicated
- ln1_shift_grad: float32 [2048], replicated
- qkv_weight_grad: float32 [3, 2048, 2048], P(None, None, 'tensor')
- qkv_bias_grad: float32 [2, 2048], P(None, 'tensor')
- out_weight_grad: float32 [2048, 2048], P('tensor')
- out_bias_grad: float32 [2048], replicated
- ln2_gain_grad: float32 [2048], replicated
- ln2_shift_grad: float32 [2048], replicated
- up_weight_grad: float32 [2048, 8192], P(None, 'tensor')
- up_bias_grad: float32 [8192], P('tensor')
- down_weight_grad: float32 [8192, 2048], P('tensor')
- down_bias_grad: float32 [2048], replicated
Inputs may be any that keep to these rules, and one draw needn't show every extreme that they name: A sequence's valid tokens are its first lengths[s] slots; some sequence has exactly 1024 and some exactly 256.
All inputs are finite; a program needn't handle non-finite values.
Results may differ from a plain program's by a relative error of at most 0.018.
Values may be sent and summed in bfloat16 or wider, within the bound.
A program may use at most 256 MiB of HBM per device.

v0:
```python
import jax
import jax.numpy as jnp
from jax import lax
from jax.sharding import PartitionSpec as P

HD = 128
norm_epsilon = 1e-05
block_rows = 512


def layer_norm(values, norm_gain, norm_shift):
    centre = values - jnp.mean(values, axis=-1, keepdims=True)
    spread = jnp.mean(centre * centre, axis=-1, keepdims=True)
    return centre * lax.rsqrt(spread + norm_epsilon) * norm_gain + norm_shift


def gelu_exact(values):
    return jax.nn.gelu(values, approximate=False)


def flat_product(left_rows, right_rows):
    flat = left_rows.reshape(-1, left_rows.shape[-1])
    result = jnp.dot(flat, right_rows, preferred_element_type=jnp.float32)
    return result.reshape(left_rows.shape[:-1] + (right_rows.shape[-1],))


def product_back(left_rows, right_rows):
    flat = left_rows.reshape(-1, left_rows.shape[-1])
    result = lax.dot_general(
        flat, right_rows, (((1,), (1,)), ((), ())), preferred_element_type=jnp.float32
    )
    return result.reshape(left_rows.shape[:-1] + (right_rows.shape[0],))


def rows_product(left_rows, right_rows):
    left_flat = left_rows.reshape(-1, left_rows.shape[-1])
    right_flat = right_rows.reshape(-1, right_rows.shape[-1])
    return lax.dot_general(
        left_flat, right_flat, (((0,), (0,)), ((), ())), preferred_element_type=jnp.float32
    )


def allowed_mask(first_row, row_count, slot_count, length):
    row_ids = first_row + lax.broadcasted_iota(jnp.int32, (row_count, slot_count), 0)
    col_ids = lax.broadcasted_iota(jnp.int32, (row_count, slot_count), 1)
    return (col_ids <= row_ids) & (col_ids < length)


def block_scores(query_block, key_rows, first_row, length):
    scores = jnp.einsum("qhd,khd->hqk", query_block, key_rows, preferred_element_type=jnp.float32)
    allowed = allowed_mask(first_row, query_block.shape[0], key_rows.shape[0], length)
    return jnp.where(allowed[None], scores, -1e30)


def attend_forward(query_rows, key_rows, value_rows, length):
    slot_count = query_rows.shape[0]
    step_rows = min(block_rows, slot_count)
    outputs = []
    totals = []
    for block_index in range(slot_count // step_rows):
        first_row = block_index * step_rows
        query_block = query_rows[first_row : first_row + step_rows]
        scores = block_scores(query_block, key_rows, first_row, length)
        row_peak = jnp.max(scores, axis=-1, keepdims=True)
        log_total = row_peak + jnp.log(jnp.sum(jnp.exp(scores - row_peak), axis=-1, keepdims=True))
        weights = jnp.exp(scores - log_total).astype(jnp.bfloat16)
        outputs.append(
            jnp.einsum("hqk,khd->qhd", weights, value_rows, preferred_element_type=jnp.float32)
        )
        totals.append(log_total)
    return (jnp.concatenate(outputs, axis=0), jnp.concatenate(totals, axis=1))


def attend_backward(query_rows, key_rows, value_rows, grad_rows, log_totals, length):
    slot_count = query_rows.shape[0]
    step_rows = min(block_rows, slot_count)
    grad_keys = jnp.zeros(key_rows.shape, jnp.float32)
    grad_values = jnp.zeros(value_rows.shape, jnp.float32)
    grad_queries = []
    for block_index in range(slot_count // step_rows):
        first_row = block_index * step_rows
        query_block = query_rows[first_row : first_row + step_rows]
        grad_block = grad_rows[first_row : first_row + step_rows]
        scores = block_scores(query_block, key_rows, first_row, length)
        probs = jnp.exp(scores - log_totals[:, first_row : first_row + step_rows])
        grad_probs = jnp.einsum(
            "qhd,khd->hqk", grad_block, value_rows, preferred_element_type=jnp.float32
        )
        centre = jnp.sum(probs * grad_probs, axis=-1, keepdims=True)
        grad_scores = (probs * (grad_probs - centre)).astype(jnp.bfloat16)
        grad_queries.append(
            jnp.einsum("hqk,khd->qhd", grad_scores, key_rows, preferred_element_type=jnp.float32)
        )
        grad_keys = grad_keys + jnp.einsum(
            "hqk,qhd->khd", grad_scores, query_block, preferred_element_type=jnp.float32
        )
        grad_values = grad_values + jnp.einsum(
            "hqk,qhd->khd",
            probs.astype(jnp.bfloat16),
            grad_block,
            preferred_element_type=jnp.float32,
        )
    return (jnp.concatenate(grad_queries, axis=0), grad_keys, grad_values)


def body(
    tokens,
    cotangent,
    lengths,
    ln1_gain,
    ln1_shift,
    qkv_weight,
    qkv_bias,
    out_weight,
    out_bias,
    ln2_gain,
    ln2_shift,
    up_weight,
    up_bias,
    down_weight,
    down_bias,
):
    seq_count, local_rows, model_width = tokens.shape
    part_width = qkv_weight.shape[2]
    head_count = part_width // HD
    score_scale = HD ** (-0.5)
    inputs = tokens.astype(jnp.float32)
    normed_one = layer_norm(inputs, ln1_gain, ln1_shift).astype(jnp.bfloat16)
    gathered_one = lax.all_gather(normed_one, "tensor", axis=1, tiled=True)
    slot_count = gathered_one.shape[1]
    head_shape = (seq_count, slot_count, head_count, HD)
    query_rows = (
        ((flat_product(gathered_one, qkv_weight[0]) + qkv_bias[0]) * score_scale)
        .astype(jnp.bfloat16)
        .reshape(head_shape)
    )
    key_rows = flat_product(gathered_one, qkv_weight[1]).astype(jnp.bfloat16).reshape(head_shape)
    value_rows = (
        (flat_product(gathered_one, qkv_weight[2]) + qkv_bias[1])
        .astype(jnp.bfloat16)
        .reshape(head_shape)
    )
    attended, log_totals = lax.map(
        lambda item: attend_forward(item[0], item[1], item[2], item[3]),
        (query_rows, key_rows, value_rows, lengths),
    )
    mixed_heads = attended.reshape(seq_count, slot_count, part_width).astype(jnp.bfloat16)
    attn_local = lax.psum_scatter(
        flat_product(mixed_heads, out_weight).astype(jnp.bfloat16),
        "tensor",
        scatter_dimension=1,
        tiled=True,
    ).astype(jnp.float32)
    hidden_state = inputs + attn_local + out_bias
    normed_two = layer_norm(hidden_state, ln2_gain, ln2_shift).astype(jnp.bfloat16)
    gathered_two = lax.all_gather(normed_two, "tensor", axis=1, tiled=True)
    pre_act = flat_product(gathered_two, up_weight) + up_bias
    activated = gelu_exact(pre_act).astype(jnp.bfloat16)
    mlp_local = lax.psum_scatter(
        flat_product(activated, down_weight).astype(jnp.bfloat16),
        "tensor",
        scatter_dimension=1,
        tiled=True,
    ).astype(jnp.float32)
    output = (hidden_state + mlp_local + down_bias).astype(jnp.bfloat16)
    slot_ids = lax.axis_index("tensor") * local_rows + lax.broadcasted_iota(
        jnp.int32, (seq_count, local_rows), 1
    )
    valid_rows = (slot_ids < lengths[:, None]).astype(jnp.float32)
    grad_out = cotangent.astype(jnp.float32) * valid_rows[:, :, None]
    down_bias_grad = jnp.sum(grad_out, axis=(0, 1))
    grad_mlp = lax.all_gather(grad_out.astype(jnp.bfloat16), "tensor", axis=1, tiled=True)
    down_weight_grad = rows_product(activated, grad_mlp)
    grad_act = product_back(grad_mlp, down_weight)
    unused_act, gelu_back = jax.vjp(gelu_exact, pre_act)
    grad_pre = gelu_back(grad_act)[0].astype(jnp.bfloat16)
    up_bias_grad = jnp.sum(grad_pre.astype(jnp.float32), axis=(0, 1))
    up_weight_grad = rows_product(gathered_two, grad_pre)
    norm_two_grad = lax.psum_scatter(
        product_back(grad_pre, up_weight), "tensor", scatter_dimension=1, tiled=True
    )
    unused_two, norm_two_back = jax.vjp(layer_norm, hidden_state, ln2_gain, ln2_shift)
    hidden_ln_grad, ln2_gain_grad, ln2_shift_grad = norm_two_back(norm_two_grad)
    hidden_grad = grad_out + hidden_ln_grad
    out_bias_grad = jnp.sum(hidden_grad, axis=(0, 1))
    grad_attn = lax.all_gather(hidden_grad.astype(jnp.bfloat16), "tensor", axis=1, tiled=True)
    out_weight_grad = rows_product(mixed_heads, grad_attn)
    grad_heads = product_back(grad_attn, out_weight).astype(jnp.bfloat16).reshape(head_shape)
    grad_query, grad_key, grad_value = lax.map(
        lambda item: attend_backward(item[0], item[1], item[2], item[3], item[4], item[5]),
        (query_rows, key_rows, value_rows, grad_heads, log_totals, lengths),
    )
    flat_shape = (seq_count, slot_count, part_width)
    grad_query = grad_query.reshape(flat_shape).astype(jnp.bfloat16)
    grad_key = grad_key.reshape(flat_shape).astype(jnp.bfloat16)
    grad_value = grad_value.reshape(flat_shape).astype(jnp.bfloat16)
    qkv_weight_grad = jnp.stack(
        [
            score_scale * rows_product(gathered_one, grad_query),
            rows_product(gathered_one, grad_key),
            rows_product(gathered_one, grad_value),
        ]
    )
    qkv_bias_grad = jnp.stack(
        [
            score_scale * jnp.sum(grad_query.astype(jnp.float32), axis=(0, 1)),
            jnp.sum(grad_value.astype(jnp.float32), axis=(0, 1)),
        ]
    )
    norm_one_part = (
        score_scale * product_back(grad_query, qkv_weight[0])
        + product_back(grad_key, qkv_weight[1])
        + product_back(grad_value, qkv_weight[2])
    )
    norm_one_grad = lax.psum_scatter(norm_one_part, "tensor", scatter_dimension=1, tiled=True)
    unused_one, norm_one_back = jax.vjp(layer_norm, inputs, ln1_gain, ln1_shift)
    input_ln_grad, ln1_gain_grad, ln1_shift_grad = norm_one_back(norm_one_grad)
    input_grad = hidden_grad + input_ln_grad
    (
        qkv_weight_grad,
        qkv_bias_grad,
        out_weight_grad,
        up_weight_grad,
        up_bias_grad,
        down_weight_grad,
    ) = lax.psum(
        (
            qkv_weight_grad,
            qkv_bias_grad,
            out_weight_grad,
            up_weight_grad,
            up_bias_grad,
            down_weight_grad,
        ),
        "dp",
    )
    ln1_gain_grad, ln1_shift_grad, out_bias_grad, ln2_gain_grad, ln2_shift_grad, down_bias_grad = (
        lax.psum(
            (
                ln1_gain_grad,
                ln1_shift_grad,
                out_bias_grad,
                ln2_gain_grad,
                ln2_shift_grad,
                down_bias_grad,
            ),
            ("dp", "tensor"),
        )
    )
    return (
        output,
        input_grad,
        ln1_gain_grad,
        ln1_shift_grad,
        qkv_weight_grad,
        qkv_bias_grad,
        out_weight_grad,
        out_bias_grad,
        ln2_gain_grad,
        ln2_shift_grad,
        up_weight_grad,
        up_bias_grad,
        down_weight_grad,
        down_bias_grad,
    )


def solution(mesh):
    in_specs = (
        P("dp", "tensor", None),
        P("dp", "tensor", None),
        P("dp"),
        P(),
        P(),
        P(None, None, "tensor"),
        P(None, "tensor"),
        P("tensor", None),
        P(),
        P(),
        P(),
        P(None, "tensor"),
        P("tensor"),
        P("tensor", None),
        P(),
    )
    out_specs = (
        P("dp", "tensor", None),
        P("dp", "tensor", None),
        P(),
        P(),
        P(None, None, "tensor"),
        P(None, "tensor"),
        P("tensor", None),
        P(),
        P(),
        P(),
        P(None, "tensor"),
        P("tensor"),
        P("tensor", None),
        P(),
    )
    return jax.shard_map(body, mesh=mesh, in_specs=in_specs, out_specs=out_specs, check_vma=False)
```

profile of v0, /device:TPU:0, one launch (start us, length us, event | category | flops | bytes accessed | tf_op | source)
XLA Modules:
  0.0 1510.5 jit_solution(7519367030076174390)
XLA Ops:
  13.2 84.8 %all-gather.5.cloned.1.call-done = bf16[2,1024,2048]{2,1,0:T(8,128)(2,1)} async-done(((bf16[2,128,2048]{2,1,0:T(8,128)(2,1)}), bf16[2,1024,2048]{2,1,0:T(8,128)(2,1)}) %all-gather.5.cloned.1.call-update) | async-done | bytes 8388624 | tf_op jit(solution)/shard_map/all_gather | solution.py:129
  121.9 19.5 %while.26 = (s32[]{:T(128)}, bf16[2,1024,2,128]{1,3,2,0:T(8,128)(2,1)}, f32[2,2,1024,1]{2,1,3,0:T(2,128)S(1)}, bf16[2,1024,2,128]{1,3,2,0:T(8,128)(2,1)}, s32[2]...) while((s32[]{:T(128)}, ...), condition=%wide.region_7.8_spmd, body=%wide.region_2.7_spmd.sunk | while | flops 1093666304 | bytes 46220012 | solution.py:143
  141.4 7.4 convolution_convert_fusion.1
  148.9 88.2 %reduce-scatter.5.cloned.1.call-done = bf16[2,128,2048]{2,1,0:T(8,128)(2,1)} async-done(((bf16[2,1024,2048]{2,1,0:T(8,128)(2,1)}), bf16[2,128,2048]{2,1,0:T(8,128)(2,1)}) %reduce-scatter.5.cloned.1.call-update) | async-done | bytes 1048592 | tf_op jit(solution)/shard_map/reduce_scatter | solution.py:148
  245.1 77.9 %all-gather.7.cloned.1.call-done = bf16[2,1024,2048]{2,1,0:T(8,128)(2,1)} async-done(((bf16[2,128,2048]{2,1,0:T(8,128)(2,1)}), bf16[2,1024,2048]{2,1,0:T(8,128)(2,1)}) %all-gather.7.cloned.1.call-update) | async-done | bytes 8388624 | tf_op jit(solution)/shard_map/all_gather | solution.py:156
  323.0 15.6 %fusion.114 = (u8[1024,1024]{1,0:T(8,128)(4,1)S(1)}, u8[1024,1024]{1,0:T(8,128)(4,1)S(1)}, f32[2,1024,1024]{2,1,0:T(8,128)S(1)}) fusion(f32[1024]{0:T(1024)S(1)} %copy-done.47, bf16[2,1024,2048]{2,1,0:T(8,128)(2,1)} %all-gather.7.cloned.1.call-done, bf16[2048,1024]{1,0:T(8,128)(2,1)} %param.30), kind=kOutput, calls=%fused_computation.186 | convolution fusion | flops 8617197568 | bytes 23072768 | tf_op jit(solution)/shard_map/dot_general | solution.py:23
  342.0 20.5 %multiply_convert_fusion.2 = (bf16[2,1024,1024]{2,1,0:T(8,128)(2,1)}, f32[2,1024,1024]{2,1,0:T(8,128)}) fusion(f32[2,1024,1024]{2,1,0:T(8,128)S(1)} %get-tuple-element.211, f32[1024]{0:T(1024)S(1)} %copy-done.47, u8[1024,1024]{1,0:T(8,128)(4,1)S(1)} %get-tuple-element.129, u8[1024,1024]{1,0:T(8,128)(4,1)S(1)} %get-tuple-element.128), kind=kLoop, calls=%fused_computation.124 | loop fusion | flops 148897792 | bytes 23072768 | tf_op jit(solution)/shard_map/convert_element_type | solution.py:158
  362.6 43.1 %all-gather.9.cloned.1.call-done = bf16[2,1024,2048]{2,1,0:T(8,128)(2,1)} async-done(((bf16[2,128,2048]{2,1,0:T(8,128)(2,1)}), bf16[2,1024,2048]{2,1,0:T(8,128)(2,1)}) %all-gather.9.cloned.1.call-update) | async-done | bytes 8388624 | tf_op jit(solution)/shard_map/all_gather | solution.py:172
  405.6 21.2 %convert_reduce_fusion = (f32[1024]{0:T(1024)}, bf16[2,1024,1024]{2,1,0:T(8,128)(2,1)S(1)}) fusion(f32[2,1024,1024]{2,1,0:T(8,128)} %get-tuple-element.188, bf16[2,1024,2048]{2,1,0:T(8,128)(2,1)} %all-gather.9.cloned.1.call-done, bf16[1024,2048]{1,0:T(8,128)(2,1)} %param.32, f32[2,1024,1024]{2,1,0:T(8,128)} %copy-done.20, f32[1024]{0:T(1024)S(1)} %copy-done.47), kind=kOutput, calls=%fused_computation.122 | convolution fusion | flops 8625585152 | bytes 33562624 | tf_op jit(solution)/shard_map/dot_general | solution.py:29
  428.8 11.7 fusion.93
  440.6 14.3 convolution_convert_fusion
  455.0 152.5 %reduce-scatter.9.cloned.1.call-done = f32[2,128,2048]{2,1,0:T(8,128)} async-done(((f32[2,1024,2048]{2,1,0:T(8,128)}), f32[2,128,2048]{2,1,0:T(8,128)}) %reduce-scatter.9.cloned.1.call-update) | async-done | bytes 2097168 | tf_op jit(solution)/shard_map/reduce_scatter | solution.py:179
  611.0 87.2 %reduce-scatter.7.cloned.1.call-done = bf16[2,128,2048]{2,1,0:T(8,128)(2,1)} async-done(((bf16[2,1024,2048]{2,1,0:T(8,128)(2,1)}), bf16[2,128,2048]{2,1,0:T(8,128)(2,1)}) %reduce-scatter.7.cloned.1.call-update) | async-done | bytes 1048592 | tf_op jit(solution)/shard_map/reduce_scatter | solution.py:159
  705.2 80.5 %all-gather.11.cloned.1.call-done = bf16[2,1024,2048]{2,1,0:T(8,128)(2,1)} async-done(((bf16[2,128,2048]{2,1,0:T(8,128)(2,1)}), bf16[2,1024,2048]{2,1,0:T(8,128)(2,1)}) %all-gather.11.cloned.1.call-update) | async-done | bytes 8388624 | tf_op jit(solution)/shard_map/all_gather | solution.py:186
  795.8 33.9 %while.27 = (s32[]{:T(128)}, bf16[2,1024,2,128]{1,3,2,0:T(8,128)(2,1)}, bf16[2,1024,2,128]{1,3,2,0:T(8,128)(2,1)}, bf16[2,1024,2,128]{1,3,2,0:T(8,128)(2,1)}, bf...) while((s32[]{:T(128)}, ...), condition=%wide.region_18.19_spmd, body=%wide.region_15.18_spmd.sunk | while | flops 2713189888 | bytes 113858456 | solution.py:189
  829.7 9.8 fusion.120
  839.4 9.5 fusion.117
  848.9 18.5 %add_add_fusion = f32[2,1024,2048]{2,1,0:T(8,128)} fusion(f32[2,1024,2048]{2,1,0:T(8,128)} %fusion.117, f32[2,1024,2048]{2,1,0:T(8,128)} %fusion.120, bf16[2,1024,256]{1,2,0:T(8,128)(2,1)S(1)} %bitcast.299, bf16[3,2048,256]{2,1,0:T(8,128)(2,1)} %param.24), kind=kOutput, calls=%fused_computation.114 | convolution fusion | flops 2160066560 | bytes 52428800 | tf_op jit(solution)/shard_map/dot_general | solution.py:29
  867.4 15.0 convolution_bitcast_fusion.3
  882.5 14.0 convolution_bitcast_fusion.2
  919.5 10.8 all-reduce.1
  930.3 104.0 %reduce-scatter.11.cloned.1.call-done = f32[2,128,2048]{2,1,0:T(8,128)} async-done(((f32[2,1024,2048]{2,1,0:T(8,128)}), f32[2,128,2048]{2,1,0:T(8,128)}) %reduce-scatter.11.cloned.1.call-update) | async-done | bytes 2097168 | tf_op jit(solution)/shard_map/reduce_scatter | solution.py:215
  1041.8 39.5 %all-reduce = (f32[2048]{0:T(1024)}, f32[2048]{0:T(1024)}, f32[2048]{0:T(1024)}, f32[2048]{0:T(1024)}, f32[2048]{0:T(1024)}, /*index=5*/f32[2048]{0:T(1024)}) all-reduce(f32[2048]{0:T(1024)S(1)} %get-tuple-element.132, f32[2048]{0:T(1024)S(1)} %get-tuple-element.135, ...), channel_id=1, replica_groups=mesh['dp'=4,'tensor'=8] {'dp','tensor'}, use_global_device_ids=true, to_apply=%region_23.24 | all-reduce | flops 12288 | bytes 98304 | tf_op jit(solution)/shard_map/psum | solution.py:238
  1081.3 404.6 %all-reduce.5.cloned.1.call-done = (f32[3,2048,256]{2,1,0:T(8,128)}, f32[256,2048]{1,0:T(8,128)}, f32[2048,1024]{1,0:T(8,128)}, f32[1024,2048]{1,0:T(8,128)}) async-done(((f32[3,2048,256]{2,1,0:T(8,128)}, f32[256,2048]{1,0:T(8,128)}, f32[2048,1024]{1,0:T(8,128)}, f32[1024,2048]{1,0:T(8,128)}), (f32[3,2048,256]{2,1,0:T(8,128)}, f32[256,2048]{1,0:T(8,128)}, f32[2048,1024]{1,0:T(8,128)}, ...) | async-done | bytes 25165840 | tf_op jit(solution)/shard_map/psum | solution.py:226
  (270 shorter events, 164.1 us)
Async XLA Ops:
  7.2 134.2 %copy-start = (bf16[256,2048]{1,0:T(8,128)(2,1)S(1)}, bf16[256,2048]{1,0:T(8,128)(2,1)}, u32[]{:S(2)}) copy-start(bf16[256,2048]{1,0:T(8,128)(2,1)} %param.26) | copy-start | bytes 3145732
  7.2 90.9 %all-gather.5.cloned.1.call-start = ((), (), s32[]{:S(2)}) async-start(), calls=%async_computation.4 | async-start | bytes 9437184 | tf_op jit(solution)/shard_map/all_gather | solution.py:129
  13.2 224.0 %reduce-scatter.5.cloned.1.call-start = ((), (), s32[]{:S(2)}) async-start(), calls=%async_computation.5 | async-start | bytes 9437184 | tf_op jit(solution)/shard_map/reduce_scatter | solution.py:148
  148.8 91.9 %copy-start.32 = (f32[2048]{0:T(1024)S(1)}, f32[2048]{0:T(1024)}, u32[]{:S(2)}) copy-start(f32[2048]{0:T(1024)} %param.28) | copy-start | bytes 24580
  148.9 91.9 %copy-start.45 = (f32[2048]{0:T(1024)S(1)}, f32[2048]{0:T(1024)}, u32[]{:S(2)}) copy-start(f32[2048]{0:T(1024)} %param.29) | copy-start | bytes 24580
  148.9 174.1 %all-gather.7.cloned.1.call-start = ((), (), s32[]{:S(2)}) async-start(), calls=%async_computation.6 | async-start | bytes 9437184 | tf_op jit(solution)/shard_map/all_gather | solution.py:156
  242.4 163.2 %all-gather.9.cloned.1.call-start = ((), (), s32[]{:S(2)}) async-start(), calls=%async_computation.8 | async-start | bytes 9437184 | tf_op jit(solution)/shard_map/all_gather | solution.py:172
  242.6 460.0 %copy-start.39 = (f32[2,128]{1,0:T(2,128)}, f32[2,128]{1,0:T(2,128)S(1)}, u32[]{:S(2)}) copy-start(f32[2,128]{1,0:T(2,128)S(1)} %compare_convert_fusion) | copy-start | bytes 3076
  245.0 362.5 %reduce-scatter.9.cloned.1.call-start = ((), (), s32[]{:S(2)}) async-start(), calls=%async_computation.9 | async-start | bytes 18874368 | tf_op jit(solution)/shard_map/reduce_scatter | solution.py:179
  440.6 257.7 %reduce-scatter.7.cloned.1.call-start = ((), (), s32[]{:S(2)}) async-start(), calls=%async_computation.7 | async-start | bytes 9437184 | tf_op jit(solution)/shard_map/reduce_scatter | solution.py:159
  455.0 243.3 %copy-start.46 = (f32[2048]{0:T(1024)S(1)}, f32[2048]{0:T(1024)}, u32[]{:S(2)}) copy-start(f32[2048]{0:T(1024)} %param.33) | copy-start | bytes 24580
  455.0 330.8 %all-gather.11.cloned.1.call-start = ((), (), s32[]{:S(2)}) async-start(), calls=%async_computation.10 | async-start | bytes 9437184 | tf_op jit(solution)/shard_map/all_gather | solution.py:186
  702.5 90.0 %copy-start.43 = (f32[2,128]{1,0:T(2,128)}, f32[2,128]{1,0:T(2,128)S(1)}, u32[]{:S(2)}) copy-start(f32[2,128]{1,0:T(2,128)S(1)} %negate_multiply_fusion.2) | copy-start | bytes 3076
  705.2 329.1 %reduce-scatter.11.cloned.1.call-start = ((), (), s32[]{:S(2)}) async-start(), calls=%async_computation.11 | async-start | bytes 18874368 | tf_op jit(solution)/shard_map/reduce_scatter | solution.py:215
  705.2 90.5 %copy-start.5 = (bf16[2,1024,2,128]{3,1,2,0:T(8,128)(2,1)S(1)}, bf16[2,1024,2,128]{3,1,2,0:T(8,128)(2,1)}, u32[]{:S(2)}) copy-start(bf16[2,1024,2,128]{3,1,2,0:T(8,128)(2,1)} %copy-done.4) | copy-start | bytes 3145732
  867.4 618.6 %all-reduce.5.cloned.1.call-start = ((), (), s32[]{:S(2)}) async-start(), calls=%async_computation.12 | async-start | bytes 50331648 | tf_op jit(solution)/shard_map/psum | solution.py:226
  918.8 115.5 %copy-start.3 = (bf16[2,128,2048]{2,1,0:T(8,128)(2,1)S(1)}, bf16[2,128,2048]{2,1,0:T(8,128)(2,1)}, u32[]{:S(2)}) copy-start(bf16[2,128,2048]{2,1,0:T(8,128)(2,1)} %param.19) | copy-start | bytes 3145732
  918.8 115.5 %copy-start.31 = (f32[2048]{0:T(1024)S(1)}, f32[2048]{0:T(1024)}, u32[]{:S(2)}) copy-start(f32[2048]{0:T(1024)} %param.22) | copy-start | bytes 24580
  918.8 115.6 %copy-start.34 = (f32[2,128]{1,0:T(2,128)S(1)}, f32[2,128]{1,0:T(2,128)}, u32[]{:S(2)}) copy-start(f32[2,128]{1,0:T(2,128)} %copy-done.33) | copy-start | bytes 3076
  918.8 117.8 %copy-start.42 = (f32[2,128]{1,0:T(2,128)S(1)}, f32[2,128]{1,0:T(2,128)}, u32[]{:S(2)}) copy-start(f32[2,128]{1,0:T(2,128)} %copy-done.41) | copy-start | bytes 3076
  918.8 117.8 %copy-start.38 = (f32[2,128]{1,0:T(2,128)S(1)}, f32[2,128]{1,0:T(2,128)}, u32[]{:S(2)}) copy-start(f32[2,128]{1,0:T(2,128)} %copy-done.37) | copy-start | bytes 3076
  918.8 118.7 %copy-start.40 = (f32[2,128]{1,0:T(2,128)S(1)}, f32[2,128]{1,0:T(2,128)}, u32[]{:S(2)}) copy-start(f32[2,128]{1,0:T(2,128)} %copy-done.39) | copy-start | bytes 3076
  918.8 118.7 %copy-start.44 = (f32[2,128]{1,0:T(2,128)S(1)}, f32[2,128]{1,0:T(2,128)}, u32[]{:S(2)}) copy-start(f32[2,128]{1,0:T(2,128)} %copy-done.43) | copy-start | bytes 3076
  919.2 118.4 %copy-start.19 = (bf16[2,128,2048]{2,1,0:T(8,128)(2,1)S(1)}, bf16[2,128,2048]{2,1,0:T(8,128)(2,1)}, u32[]{:S(2)}) copy-start(bf16[2,128,2048]{2,1,0:T(8,128)(2,1)} %param.20) | copy-start | bytes 3145732
  (55 other events, 738.9 us)
Sparse Core Ops, SparseCore 0:
  13.3 84.7 all-gather.4
  149.0 88.1 reduce-scatter.4
  242.5 80.3 all-gather.6
  325.0 80.5 all-gather.8
  440.7 166.7 reduce-scatter.8
  610.2 87.9 reduce-scatter.6
  705.3 80.3 all-gather.10
  867.5 166.7 reduce-scatter.10
  1039.4 446.4 all-reduce.4
where the time goes:
time: 1510 us
  waiting for transfers between devices  1120 us (74%)
  matrix products  212 us (14%)
  other arithmetic  68.2 us (5%)
  blocking collectives  50.4 us (3%)
  local copies, waits for them, and re-layouts  40.8 us (3%)
    psum x1, waiting for transfers between devices, body(): lax.psum((qkv_weight_grad, qkv_bias_grad, out_weight_grad, up_weight_grad...  405 us
    reduce_scatter x1, waiting for transfers between devices, body(): lax.psum_scatter(product_back(grad_pre, up_weight), 'tensor', scatter_dim...  152 us
    reduce_scatter x1, waiting for transfers between devices, body(): lax.psum_scatter(norm_one_part, 'tensor', scatter_dimension=1, tiled=True)  104 us
    reduce_scatter x1, waiting for transfers between devices, body(): lax.psum_scatter(flat_product(mixed_heads, out_weight).astype(jnp.bfloat1...  88.2 us
    reduce_scatter x1, waiting for transfers between devices, body(): lax.psum_scatter(flat_product(activated, down_weight).astype(jnp.bfloat16...  87.2 us
    all_gather x1, waiting for transfers between devices, body(): gathered_one = lax.all_gather(normed_one, 'tensor', axis=1, tiled=True)  84.8 us
    all_gather x1, waiting for transfers between devices, body(): lax.all_gather(hidden_grad.astype(jnp.bfloat16), 'tensor', axis=1, tiled=...  80.5 us
    all_gather x1, waiting for transfers between devices, body(): gathered_two = lax.all_gather(normed_two, 'tensor', axis=1, tiled=True)  77.9 us
  transfers between devices with their start and end apart: 9, of which 9 were waited for; matrix products, arithmetic and copies ran while one was open for 8% of the time, Pallas kernels for 0%

commit v1 on v0

--- a/solution.py
+++ b/solution.py
@@ -6,6 +6,28 @@
 HD = 128
 norm_epsilon = 1e-05
 block_rows = 512
+
+
+def in_order(blocks, dim):
+    dims = list(blocks.shape[1:])
+    dims[dim] *= blocks.shape[0]
+    return jnp.moveaxis(blocks, 0, dim).reshape(dims)
+
+
+def doubled(array, axis):
+    peers = lax.axis_size(axis)
+    parts = array[None]
+    for level in range(peers.bit_length() - 1):
+        bit = 1 << level
+        other = lax.ppermute(parts, axis, [(i, i ^ bit) for i in range(peers)])
+        both = jnp.stack([parts, other])
+        upper = lax.axis_index(axis) >> level & 1
+        parts = jnp.where(upper == 0, both, both[::-1]).reshape(-1, *array.shape)
+    return parts
+
+
+def gather_by_bits(x, axis, dim):
+    return in_order(doubled(x, axis), dim)
 
 
 def layer_norm(values, norm_gain, norm_shift):
@@ -169,7 +191,7 @@
     valid_rows = (slot_ids < lengths[:, None]).astype(jnp.float32)
     grad_out = cotangent.astype(jnp.float32) * valid_rows[:, :, None]
     down_bias_grad = jnp.sum(grad_out, axis=(0, 1))
-    grad_mlp = lax.all_gather(grad_out.astype(jnp.bfloat16), "tensor", axis=1, tiled=True)
+    grad_mlp = gather_by_bits(grad_out.astype(jnp.bfloat16), "tensor", 1)
     down_weight_grad = rows_product(activated, grad_mlp)
     grad_act = product_back(grad_mlp, down_weight)
     unused_act, gelu_back = jax.vjp(gelu_exact, pre_act)

time: 1510 us -> 1730 us (1.15)
  waiting for transfers between devices: 1120 us -> 1300 us
  other arithmetic: 68.2 us -> 101 us
    ppermute x0 -> x3, waiting for transfers between devices: none -> 297 us  [doubled(): other = lax.ppermute(parts, axis, [(i, i ^ bit) for i in range(peers)])]
    all_gather x1, waiting for transfers between devices: 77.9 us -> 0.01 us  [body(): gathered_two = lax.all_gather(normed_two, 'tensor', axis=1, tiled=True)]
    all_gather x1 -> x0, waiting for transfers between devices: 43.1 us -> none  [body(): lax.all_gather(grad_out.astype(jnp.bfloat16), 'tensor', axis=1, tiled=True)]
    another operation x0 -> x5, other arithmetic: none -> 17.7 us  [doubled(): both = jnp.stack([parts, other])]
    select_n x0 -> x2, other arithmetic: none -> 17.5 us  [doubled(): parts = jnp.where(upper == 0, both, both[::-1]).reshape(-1, *array.shape)]
  transfers between devices with their start and end apart: 9 -> 11, of which waited for: 9 -> 10; matrix products, arithmetic and copies ran while one was open for 8% -> 7% of each run, Pallas kernels for 0% -> 0%
where the time goes in v1:
time: 1730 us
  waiting for transfers between devices  1300 us (75%)
  matrix products  214 us (12%)
  other arithmetic  101 us (6%)
  blocking collectives  50.5 us (3%)
  local copies, waits for them, and re-layouts  43.2 us (2%)
    psum x1, waiting for transfers between devices, body(): lax.psum((qkv_weight_grad, qkv_bias_grad, out_weight_grad, up_weight_grad...  405 us
    ppermute x3, waiting for transfers between devices, doubled(): other = lax.ppermute(parts, axis, [(i, i ^ bit) for i in range(peers)])  297 us
    reduce_scatter x1, waiting for transfers between devices, body(): lax.psum_scatter(product_back(grad_pre, up_weight), 'tensor', scatter_dim...  153 us
    reduce_scatter x1, waiting for transfers between devices, body(): lax.psum_scatter(norm_one_part, 'tensor', scatter_dimension=1, tiled=True)  104 us
    reduce_scatter x1, waiting for transfers between devices, body(): lax.psum_scatter(flat_product(mixed_heads, out_weight).astype(jnp.bfloat1...  88.2 us
    reduce_scatter x1, waiting for transfers between devices, body(): lax.psum_scatter(flat_product(activated, down_weight).astype(jnp.bfloat16...  87.2 us
    all_gather x1, waiting for transfers between devices, body(): gathered_one = lax.all_gather(normed_one, 'tensor', axis=1, tiled=True)  84.8 us
    all_gather x1, waiting for transfers between devices, body(): lax.all_gather(hidden_grad.astype(jnp.bfloat16), 'tensor', axis=1, tiled=...  80.5 us
  transfers between devices with their start and end apart: 11, of which 10 were waited for; matrix products, arithmetic and copies ran while one was open for 7% of the time, Pallas kernels for 0%

profile of v1, /device:TPU:0, one launch (start us, length us, event | category | flops | bytes accessed | tf_op | source)
XLA Modules:
  0.0 1725.7 jit_solution(18233081474607756860)
XLA Ops:
  13.2 84.8 %all-gather.4.cloned.1.call-done = bf16[2,1024,2048]{2,1,0:T(8,128)(2,1)} async-done(((bf16[2,128,2048]{2,1,0:T(8,128)(2,1)}), bf16[2,1024,2048]{2,1,0:T(8,128)(2,1)}) %all-gather.4.cloned.1.call-update) | async-done | bytes 8388624 | tf_op jit(solution)/shard_map/all_gather | solution.py:151
  121.6 19.5 %while.26 = (s32[]{:T(128)}, bf16[2,1024,2,128]{1,3,2,0:T(8,128)(2,1)}, f32[2,2,1024,1]{2,1,3,0:T(2,128)S(1)}, bf16[2,1024,2,128]{1,3,2,0:T(8,128)(2,1)}, s32[2]...) while((s32[]{:T(128)}, ...), condition=%wide.region_7.8_spmd, body=%wide.region_2.7_spmd.sunk | while | flops 1093666304 | bytes 46220012 | solution.py:165
  148.6 88.2 %reduce-scatter.5.cloned.1.call-done = bf16[2,128,2048]{2,1,0:T(8,128)(2,1)} async-done(((bf16[2,1024,2048]{2,1,0:T(8,128)(2,1)}), bf16[2,128,2048]{2,1,0:T(8,128)(2,1)}) %reduce-scatter.5.cloned.1.call-update) | async-done | bytes 1048592 | tf_op jit(solution)/shard_map/reduce_scatter | solution.py:170
  252.7 111.3 %collective-permute-done.1 = bf16[2,2,128,2048]{3,2,1,0:T(8,128)(2,1)} collective-permute-done((bf16[2,2,128,2048]{3,2,1,0:T(8,128)(2,1)}, bf16[2,2,128,2048]{3,2,1,0:T(8,128)(2,1)}, u32[]{:S(2)}, u32[]{:S(2)}) %collective-permute-start.1) | collective-permute-done | bytes 2097184 | tf_op jit(solution)/shard_map/ppermute | solution.py:22
  370.3 182.8 %collective-permute-done.2 = bf16[4,2,128,2048]{3,2,1,0:T(8,128)(2,1)} collective-permute-done((bf16[4,2,128,2048]{3,2,1,0:T(8,128)(2,1)}, bf16[4,2,128,2048]{3,2,1,0:T(8,128)(2,1)}, u32[]{:S(2)}, u32[]{:S(2)}) %collective-permute-start.2) | collective-permute-done | bytes 4194336 | tf_op jit(solution)/shard_map/ppermute | solution.py:22
  560.7 14.3 reverse_select_fusion
  583.3 15.9 fusion.114
  599.2 20.6 %multiply_convert_fusion.2 = (bf16[2,1024,1024]{2,1,0:T(8,128)(2,1)}, f32[2,1024,1024]{2,1,0:T(8,128)}) fusion(f32[2,1024,1024]{2,1,0:T(8,128)S(1)} %get-tuple-element.215, f32[1024]{0:T(1024)S(1)} %copy-done.46, u8[1024,1024]{1,0:T(8,128)(4,1)S(1)} %get-tuple-element.129, u8[1024,1024]{1,0:T(8,128)(4,1)S(1)} %get-tuple-element.128), kind=kLoop, calls=%fused_computation.126 | loop fusion | flops 148897792 | bytes 23072768 | tf_op jit(solution)/shard_map/convert_element_type | solution.py:180
  619.7 19.8 %convert_reduce_fusion = (f32[1024]{0:T(1024)}, bf16[2,1024,1024]{2,1,0:T(8,128)(2,1)}) fusion(f32[2,1024,1024]{2,1,0:T(8,128)} %get-tuple-element.188, bf16[2,1024,2048]{2,1,0:T(8,128)(2,1)} %bitcast.322, bf16[1024,2048]{1,0:T(8,128)(2,1)} %param.32, f32[2,1024,1024]{2,1,0:T(8,128)S(1)} %get-tuple-element.215, f32[1024]{0:T(1024)S(1)} %copy-done.46), kind=kOutput, calls=%fused_computation.124 | convolution fusion | flops 8625585152 | bytes 33562624 | tf_op jit(solution)/shard_map/dot_general | solution.py:51
  639.6 15.3 fusion.93
  655.0 14.1 convolution_convert_fusion
  669.2 153.3 %reduce-scatter.9.cloned.1.call-done = f32[2,128,2048]{2,1,0:T(8,128)} async-done(((f32[2,1024,2048]{2,1,0:T(8,128)}), f32[2,128,2048]{2,1,0:T(8,128)}) %reduce-scatter.9.cloned.1.call-update) | async-done | bytes 2097168 | tf_op jit(solution)/shard_map/reduce_scatter | solution.py:201
  826.0 87.2 %reduce-scatter.7.cloned.1.call-done = bf16[2,128,2048]{2,1,0:T(8,128)(2,1)} async-done(((bf16[2,1024,2048]{2,1,0:T(8,128)(2,1)}), bf16[2,128,2048]{2,1,0:T(8,128)(2,1)}) %reduce-scatter.7.cloned.1.call-update) | async-done | bytes 1048592 | tf_op jit(solution)/shard_map/reduce_scatter | solution.py:181
  920.2 80.5 %all-gather.8.cloned.1.call-done = bf16[2,1024,2048]{2,1,0:T(8,128)(2,1)} async-done(((bf16[2,128,2048]{2,1,0:T(8,128)(2,1)}), bf16[2,1024,2048]{2,1,0:T(8,128)(2,1)}) %all-gather.8.cloned.1.call-update) | async-done | bytes 8388624 | tf_op jit(solution)/shard_map/all_gather | solution.py:208
  1010.7 33.6 %while.27 = (s32[]{:T(128)}, bf16[2,1024,2,128]{1,3,2,0:T(8,128)(2,1)}, bf16[2,1024,2,128]{1,3,2,0:T(8,128)(2,1)}, bf16[2,1024,2,128]{1,3,2,0:T(8,128)(2,1)}, bf...) while((s32[]{:T(128)}, ...), condition=%wide.region_18.19_spmd, body=%wide.region_15.18_spmd.sunk | while | flops 2713189888 | bytes 113858456 | solution.py:211
  1044.3 9.8 fusion.122
  1054.1 9.5 fusion.119
  1063.6 18.5 %add_add_fusion = f32[2,1024,2048]{2,1,0:T(8,128)} fusion(f32[2,1024,2048]{2,1,0:T(8,128)} %fusion.119, f32[2,1024,2048]{2,1,0:T(8,128)} %fusion.122, bf16[2,1024,256]{1,2,0:T(8,128)(2,1)S(1)} %bitcast.318, bf16[3,2048,256]{2,1,0:T(8,128)(2,1)} %param.24), kind=kOutput, calls=%fused_computation.114 | convolution fusion | flops 2160066560 | bytes 52428800 | tf_op jit(solution)/shard_map/dot_general | solution.py:51
  1082.1 15.0 convolution_bitcast_fusion.2
  1097.1 13.8 fusion.146
  1133.9 11.0 all-reduce.1
  1144.9 104.2 %reduce-scatter.11.cloned.1.call-done = f32[2,128,2048]{2,1,0:T(8,128)} async-done(((f32[2,1024,2048]{2,1,0:T(8,128)}), f32[2,128,2048]{2,1,0:T(8,128)}) %reduce-scatter.11.cloned.1.call-update) | async-done | bytes 2097168 | tf_op jit(solution)/shard_map/reduce_scatter | solution.py:237
  1256.5 39.5 %all-reduce = (f32[2048]{0:T(1024)}, f32[2048]{0:T(1024)}, f32[2048]{0:T(1024)}, f32[2048]{0:T(1024)}, f32[2048]{0:T(1024)}, /*index=5*/f32[2048]{0:T(1024)}) all-reduce(f32[2048]{0:T(1024)S(1)} %get-tuple-element.132, f32[2048]{0:T(1024)S(1)} %get-tuple-element.135, ...), channel_id=1, replica_groups=mesh['dp'=4,'tensor'=8] {'dp','tensor'}, use_global_device_ids=true, to_apply=%region_23.24 | all-reduce | flops 12288 | bytes 98304 | tf_op jit(solution)/shard_map/psum | solution.py:260
  1296.0 404.6 %all-reduce.5.cloned.1.call-done = (f32[3,2048,256]{2,1,0:T(8,128)}, f32[256,2048]{1,0:T(8,128)}, f32[2048,1024]{1,0:T(8,128)}, f32[1024,2048]{1,0:T(8,128)}) async-done(((f32[3,2048,256]{2,1,0:T(8,128)}, f32[256,2048]{1,0:T(8,128)}, f32[2048,1024]{1,0:T(8,128)}, f32[1024,2048]{1,0:T(8,128)}), (f32[3,2048,256]{2,1,0:T(8,128)}, f32[256,2048]{1,0:T(8,128)}, f32[2048,1024]{1,0:T(8,128)}, ...) | async-done | bytes 25165840 | tf_op jit(solution)/shard_map/psum | solution.py:248
  (274 shorter events, 195.4 us)
Async XLA Ops:
  7.2 133.9 %copy-start = (bf16[256,2048]{1,0:T(8,128)(2,1)S(1)}, bf16[256,2048]{1,0:T(8,128)(2,1)}, u32[]{:S(2)}) copy-start(bf16[256,2048]{1,0:T(8,128)(2,1)} %param.26) | copy-start | bytes 3145732
  7.2 90.9 %all-gather.4.cloned.1.call-start = ((), (), s32[]{:S(2)}) async-start(), calls=%async_computation.4 | async-start | bytes 9437184 | tf_op jit(solution)/shard_map/all_gather | solution.py:151
  13.2 223.7 %reduce-scatter.5.cloned.1.call-start = ((), (), s32[]{:S(2)}) async-start(), calls=%async_computation.5 | async-start | bytes 9437184 | tf_op jit(solution)/shard_map/reduce_scatter | solution.py:170
  148.5 91.9 %copy-start.31 = (f32[2048]{0:T(1024)S(1)}, f32[2048]{0:T(1024)}, u32[]{:S(2)}) copy-start(f32[2048]{0:T(1024)} %param.28) | copy-start | bytes 24580
  148.6 91.8 %copy-start.44 = (f32[2048]{0:T(1024)S(1)}, f32[2048]{0:T(1024)}, u32[]{:S(2)}) copy-start(f32[2048]{0:T(1024)} %param.29) | copy-start | bytes 24580
  148.6 434.7 %all-gather.6.cloned.1.call-start = ((), (), s32[]{:S(2)}) async-start(), calls=%async_computation.6 | async-start | bytes 9437184 | tf_op jit(solution)/shard_map/all_gather | solution.py:178
  242.1 580.4 %reduce-scatter.9.cloned.1.call-start = ((), (), s32[]{:S(2)}) async-start(), calls=%async_computation.8 | async-start | bytes 18874368 | tf_op jit(solution)/shard_map/reduce_scatter | solution.py:201
  242.2 675.2 %copy-start.38 = (f32[2,128]{1,0:T(2,128)}, f32[2,128]{1,0:T(2,128)S(1)}, u32[]{:S(2)}) copy-start(f32[2,128]{1,0:T(2,128)S(1)} %compare_convert_fusion) | copy-start | bytes 3076
  245.0 3.0 collective-permute-start
  252.7 111.3 %collective-permute-start.1 = (bf16[2,2,128,2048]{3,2,1,0:T(8,128)(2,1)}, bf16[2,2,128,2048]{3,2,1,0:T(8,128)(2,1)}, u32[]{:S(2)}, u32[]{:S(2)}) collective-permute-start(bf16[2,2,128,2048]{3,2,1,0:T(8,128)(2,1)} %get-tuple-element.210), channel_id=1, source_target_pairs={{0,2},{1,3},{2,0},{3,1},{4,6},{5,7},{6,4},{7,5},{8,10},{9,11},{10,... | collective-permute-start | bytes 6291464 | tf_op jit(solution)/shard_map/ppermute | solution.py:22
  369.8 183.3 %collective-permute-start.2 = (bf16[4,2,128,2048]{3,2,1,0:T(8,128)(2,1)}, bf16[4,2,128,2048]{3,2,1,0:T(8,128)(2,1)}, u32[]{:S(2)}, u32[]{:S(2)}) collective-permute-start(bf16[4,2,128,2048]{3,2,1,0:T(8,128)(2,1)} %bitcast.50), channel_id=1, source_target_pairs={{0,4},{1,5},{2,6},{3,7},{4,0},{5,1},{6,2},{7,3},{8,12},{9,13},{10,... | collective-permute-start | bytes 12582920 | tf_op jit(solution)/shard_map/ppermute | solution.py:22
  654.9 258.3 %reduce-scatter.7.cloned.1.call-start = ((), (), s32[]{:S(2)}) async-start(), calls=%async_computation.7 | async-start | bytes 9437184 | tf_op jit(solution)/shard_map/reduce_scatter | solution.py:181
  669.1 244.0 %copy-start.45 = (f32[2048]{0:T(1024)S(1)}, f32[2048]{0:T(1024)}, u32[]{:S(2)}) copy-start(f32[2048]{0:T(1024)} %param.33) | copy-start | bytes 24580
  669.1 331.5 %all-gather.8.cloned.1.call-start = ((), (), s32[]{:S(2)}) async-start(), calls=%async_computation.9 | async-start | bytes 9437184 | tf_op jit(solution)/shard_map/all_gather | solution.py:208
  920.1 328.9 %reduce-scatter.11.cloned.1.call-start = ((), (), s32[]{:S(2)}) async-start(), calls=%async_computation.10 | async-start | bytes 18874368 | tf_op jit(solution)/shard_map/reduce_scatter | solution.py:237
  1082.1 618.6 %all-reduce.5.cloned.1.call-start = ((), (), s32[]{:S(2)}) async-start(), calls=%async_computation.11 | async-start | bytes 50331648 | tf_op jit(solution)/shard_map/psum | solution.py:248
  1133.2 115.8 %copy-start.3 = (bf16[2,128,2048]{2,1,0:T(8,128)(2,1)S(1)}, bf16[2,128,2048]{2,1,0:T(8,128)(2,1)}, u32[]{:S(2)}) copy-start(bf16[2,128,2048]{2,1,0:T(8,128)(2,1)} %param.19) | copy-start | bytes 3145732
  1133.2 115.8 %copy-start.30 = (f32[2048]{0:T(1024)S(1)}, f32[2048]{0:T(1024)}, u32[]{:S(2)}) copy-start(f32[2048]{0:T(1024)} %param.22) | copy-start | bytes 24580
  1133.2 115.8 %copy-start.33 = (f32[2,128]{1,0:T(2,128)S(1)}, f32[2,128]{1,0:T(2,128)}, u32[]{:S(2)}) copy-start(f32[2,128]{1,0:T(2,128)} %copy-done.32) | copy-start | bytes 3076
  1133.3 118.1 %copy-start.41 = (f32[2,128]{1,0:T(2,128)S(1)}, f32[2,128]{1,0:T(2,128)}, u32[]{:S(2)}) copy-start(f32[2,128]{1,0:T(2,128)} %copy-done.40) | copy-start | bytes 3076
  1133.3 118.1 %copy-start.37 = (f32[2,128]{1,0:T(2,128)S(1)}, f32[2,128]{1,0:T(2,128)}, u32[]{:S(2)}) copy-start(f32[2,128]{1,0:T(2,128)} %copy-done.36) | copy-start | bytes 3076
  1133.3 119.0 %copy-start.39 = (f32[2,128]{1,0:T(2,128)S(1)}, f32[2,128]{1,0:T(2,128)}, u32[]{:S(2)}) copy-start(f32[2,128]{1,0:T(2,128)} %copy-done.38) | copy-start | bytes 3076
  1133.3 119.0 %copy-start.43 = (f32[2,128]{1,0:T(2,128)S(1)}, f32[2,128]{1,0:T(2,128)}, u32[]{:S(2)}) copy-start(f32[2,128]{1,0:T(2,128)} %copy-done.42) | copy-start | bytes 3076
  1133.7 118.6 %copy-start.19 = (bf16[2,128,2048]{2,1,0:T(8,128)(2,1)S(1)}, bf16[2,128,2048]{2,1,0:T(8,128)(2,1)}, u32[]{:S(2)}) copy-start(bf16[2,128,2048]{2,1,0:T(8,128)(2,1)} %param.20) | copy-start | bytes 3145732
  (54 other events, 816.8 us)
Sparse Core Ops, SparseCore 0:
  13.3 84.7 all-gather.3
  148.7 88.1 reduce-scatter.4
  242.2 119.6 all-gather.5
  655.0 167.3 reduce-scatter.8
  825.2 87.9 reduce-scatter.6
  920.2 80.4 all-gather.7
  1082.2 166.7 reduce-scatter.10
  1254.1 446.5 all-reduce.4
